TPU v7x, 32 devices: a whole 2x2x4 slice. The times are simulated.
32 devices in a mesh: dp: 16 (over z, y, x), task: 2 (over core).
Axes of the slice: x: 2, y: 2, z: 4, core: 2. Of those that a mesh axis runs over, the one named last changes fastest.
Arguments:
- images: bfloat16 [64, 16, 16, 2048], P(('dp', 'task')), may hold values from -14 to 14
- bucket_shape: int32 [64, 2], P(('dp', 'task')), may hold values from 8 to 16, as said below
- pixel_mask: int32 [64, 16, 16], P(('dp', 'task')), may hold values from 0 to 1
- thresholds: int32 [64, 16, 16, 2048], P(('dp', 'task')), may hold values from 0 to 4095
- reduce_weight: bfloat16 [2048, 512], replicated, may hold values from -0.125 to 0.125
- spatial_weight: bfloat16 [9, 512, 512], replicated, may hold values from -0.09375 to 0.09375
- expand_weight: bfloat16 [512, 2048], replicated, may hold values from -0.25 to 0.25
- mid_gains: float32 [2, 512], replicated, may hold values from 0.5 to 2
- mid_biases: float32 [2, 512], replicated, may hold values from -1 to 1
- out_gain: float32 [2048], replicated, may hold values from 0.5 to 2
- out_bias: float32 [2048], replicated, may hold values from -1 to 1
- head_weights: bfloat16 [2048, 3, 2048], P(None, None, 'task'), may hold values from -0.125 to 0.125
- head_cotangent: bfloat16 [64, 16, 16, 3, 2048], P('dp', None, None, None, 'task'), may hold values from -6 to 6
Outputs:
- head_output: bfloat16 [64, 16, 16, 3, 2048], P('dp', None, None, None, 'task')
- images_grad: float32 [64, 16, 16, 2048], P(('dp', 'task'))
- reduce_grad: float32 [2048, 512], P(('dp', 'task'))
- spatial_grad: float32 [9, 512, 512], P(None, ('dp', 'task'))
- expand_grad: float32 [512, 2048], P(('dp', 'task'))
- gains_grad: float32 [2, 512], replicated
- biases_grad: float32 [2, 512], replicated
- outgain_grad: float32 [2048], replicated
- outbias_grad: float32 [2048], replicated
- heads_grad: float32 [2048, 3, 2048], P('dp', None, 'task')
Inputs may be any that keep to these rules, and one draw needn't show every extreme that they name: `bucket_shape`: each image's valid rows and columns, from a few aspect buckets; an image's valid region is the top left corner of its grid.
All inputs are finite; a program needn't handle non-finite values.
Results may differ from a plain program's by a relative error of at most 0.015.
Values may be sent and summed in bfloat16 or wider, within the bound.
No kernel may reach another device: no remote copies, remote signals or barrier semaphores. Data moves between devices by JAX's collectives and lax.ppermute only.
A program may use at most 192 MiB of HBM per device.

v0:
```python
import jax
import jax.numpy as jnp
from jax import lax
from jax.sharding import PartitionSpec as P

epsilon = 1e-05
steepness = 6.0
levels = 4096.0


def cut_along(value, dim, peers):
    shape = value.shape
    tiles = value.reshape(*shape[:dim], peers, shape[dim] // peers, *shape[dim + 1 :])
    return jnp.moveaxis(tiles, dim, 0)


def sent_and_summed(value, axis, dim):
    peers = lax.axis_size(axis)
    tiles = lax.all_to_all(cut_along(value, dim, peers), axis, 0, 0, tiled=True)
    return jnp.sum(tiles.astype(jnp.float32), axis=0)


def validity(bucket_shape, pixel_mask):
    row_index = lax.broadcasted_iota(jnp.int32, pixel_mask.shape, 1)
    col_index = lax.broadcasted_iota(jnp.int32, pixel_mask.shape, 2)
    inside = (row_index < bucket_shape[:, 0][:, None, None]) & (
        col_index < bucket_shape[:, 1][:, None, None]
    )
    return jnp.where(inside, pixel_mask, 0).astype(jnp.float32)


def inner_rows(left, right):
    return lax.dot_general(
        left, right, (((0,), (0,)), ((), ())), preferred_element_type=jnp.float32
    )


def outer_back(left, right):
    return lax.dot_general(
        left, right, (((1,), (1,)), ((), ())), preferred_element_type=jnp.float32
    )


def silu_slope(values):
    sigma = jax.nn.sigmoid(values)
    return sigma * (1.0 + values * (1.0 - sigma))


def moments(values, valid_cells):
    first, valid_count = lax.psum(
        (jnp.sum(valid_cells * values, axis=0), jnp.sum(valid_cells)), ("dp", "task")
    )
    center = first / valid_count
    deviation = values - center
    variance = (
        lax.psum(jnp.sum(valid_cells * deviation * deviation, axis=0), ("dp", "task")) / valid_count
    )
    inverse_std = lax.rsqrt(variance + epsilon)
    return ((values - center) * inverse_std, inverse_std, valid_count)


def norm_back(grad_shifted, normed, inverse_std, gain, valid_cells, valid_count):
    bias_grad, gain_grad = lax.psum(
        (jnp.sum(grad_shifted, axis=0), jnp.sum(grad_shifted * normed, axis=0)), ("dp", "task")
    )
    grad_values = (
        gain
        * inverse_std
        * (grad_shifted - valid_cells * (bias_grad + normed * gain_grad) / valid_count)
    )
    return (grad_values.astype(jnp.bfloat16), gain_grad, bias_grad)


def patches(acts):
    grid_side = acts.shape[1]
    padded = jnp.pad(acts, ((0, 0), (1, 1), (1, 1), (0, 0)))
    windows = []
    for offset in range(9):
        row_shift = offset // 3
        col_shift = offset % 3
        windows.append(
            padded[:, row_shift : row_shift + grid_side, col_shift : col_shift + grid_side, :]
        )
    return jnp.concatenate(windows, axis=-1).reshape(-1, 9 * acts.shape[-1])


def unpatch(grad_cols, image_count, grid_side, channels):
    blocks = grad_cols.reshape(image_count, grid_side, grid_side, 9, channels)
    result = jnp.zeros((image_count, grid_side + 2, grid_side + 2, channels), jnp.float32)
    for offset in range(9):
        row_shift = offset // 3
        col_shift = offset % 3
        result = result + jnp.pad(
            blocks[:, :, :, offset, :],
            ((0, 0), (row_shift, 2 - row_shift), (col_shift, 2 - col_shift), (0, 0)),
        )
    return result[:, 1 : grid_side + 1, 1 : grid_side + 1, :]


def on_device(
    images,
    bucket_shape,
    pixel_mask,
    thresholds,
    reduce_weight,
    spatial_weight,
    expand_weight,
    mid_gains,
    mid_biases,
    out_gain,
    out_bias,
    head_weights,
    head_cotangent,
):
    image_count = images.shape[0]
    grid_side = images.shape[1]
    width = images.shape[3]
    middle = reduce_weight.shape[1]
    head_count = head_weights.shape[1]
    pixels = image_count * grid_side * grid_side
    valid_cells = validity(bucket_shape, pixel_mask).reshape(pixels, 1)
    inputs = images.reshape(pixels, width)
    masked = inputs * valid_cells.astype(jnp.bfloat16)
    pre_reduce = jnp.dot(masked, reduce_weight, preferred_element_type=jnp.float32)
    normed_reduce, inverse_reduce, valid_count = moments(pre_reduce, valid_cells)
    shifted_reduce = mid_gains[0] * normed_reduce + mid_biases[0]
    act_reduce = (valid_cells * jax.nn.silu(shifted_reduce)).astype(jnp.bfloat16)
    patches_flat = patches(act_reduce.reshape(image_count, grid_side, grid_side, middle))
    spatial_flat = spatial_weight.reshape(9 * middle, middle)
    pre_spatial = jnp.dot(patches_flat, spatial_flat, preferred_element_type=jnp.float32)
    normed_spatial, inverse_spatial, _ = moments(pre_spatial, valid_cells)
    shifted_spatial = mid_gains[1] * normed_spatial + mid_biases[1]
    act_spatial = (valid_cells * jax.nn.silu(shifted_spatial)).astype(jnp.bfloat16)
    pre_expand = jnp.dot(act_spatial, expand_weight, preferred_element_type=jnp.float32)
    normed_expand, inverse_expand, _ = moments(pre_expand, valid_cells)
    residual = inputs.astype(jnp.float32) + out_gain * normed_expand + out_bias
    features = (valid_cells * jax.nn.silu(residual)).astype(jnp.bfloat16)
    gathered = lax.all_gather(
        features.reshape(image_count, grid_side, grid_side, width), "task", axis=0, tiled=True
    )
    group_images = gathered.shape[0]
    group_pixels = group_images * grid_side * grid_side
    flat_features = gathered.reshape(group_pixels, width)
    head_values = jnp.einsum(
        "pc,ctd->ptd", flat_features, head_weights, preferred_element_type=jnp.float32
    )
    head_output = head_values.astype(jnp.bfloat16).reshape(
        group_images, grid_side, grid_side, head_count, -1
    )
    sliced = head_cotangent
    task_grad = lax.psum_scatter(
        jnp.einsum(
            "ihwtd,ctd->ihwtc", sliced, head_weights, preferred_element_type=jnp.float32
        ).astype(jnp.bfloat16),
        "task",
        scatter_dimension=0,
        tiled=True,
    ).astype(jnp.float32)
    task_grad = task_grad.reshape(pixels, head_count, width)
    flat_cotangent = head_cotangent.reshape(group_pixels, head_count, -1)
    sliced = flat_features
    heads_grad = sent_and_summed(
        jnp.einsum(
            "pc,ptd->ctd", sliced, flat_cotangent, preferred_element_type=jnp.float32
        ).astype(jnp.bfloat16),
        "dp",
        0,
    )
    task_total = jnp.sum(task_grad, axis=1)
    spread = jnp.sum(jnp.sqrt(task_grad * task_grad + 1.0), axis=1)
    purity = 0.5 * (1.0 + task_total / spread)
    threshold_level = (thresholds.reshape(pixels, width).astype(jnp.float32) + 0.5) / levels
    kept_share = jax.nn.sigmoid(
        steepness * jnp.tanh(task_grad) * (purity - threshold_level)[:, None, :]
    )
    merged = jnp.sum(kept_share * task_grad, axis=1)
    grad_residual = merged * valid_cells * silu_slope(residual)
    grad_expand, outgain_grad, outbias_grad = norm_back(
        grad_residual, normed_expand, inverse_expand, out_gain, valid_cells, valid_count
    )
    expand_part = inner_rows(act_spatial, grad_expand)
    grad_act_spatial = outer_back(grad_expand, expand_weight)
    grad_spatial, gain_two, bias_two = norm_back(
        grad_act_spatial * valid_cells * silu_slope(shifted_spatial),
        normed_spatial,
        inverse_spatial,
        mid_gains[1],
        valid_cells,
        valid_count,
    )
    spatial_part = inner_rows(patches_flat, grad_spatial).reshape(9, middle, middle)
    grad_cols = outer_back(grad_spatial, spatial_flat)
    grad_act_reduce = unpatch(grad_cols, image_count, grid_side, middle).reshape(pixels, middle)
    grad_reduce, gain_one, bias_one = norm_back(
        grad_act_reduce * valid_cells * silu_slope(shifted_reduce),
        normed_reduce,
        inverse_reduce,
        mid_gains[0],
        valid_cells,
        valid_count,
    )
    reduce_part = inner_rows(masked, grad_reduce)
    images_grad = grad_residual + valid_cells * outer_back(grad_reduce, reduce_weight)
    reduce_part, spatial_part, expand_part = (
        lax.psum_scatter(reduce_part, ("dp", "task"), scatter_dimension=0, tiled=True),
        lax.psum_scatter(spatial_part, ("dp", "task"), scatter_dimension=1, tiled=True),
        lax.psum_scatter(expand_part, ("dp", "task"), scatter_dimension=0, tiled=True),
    )
    gains_grad = jnp.stack([gain_one, gain_two], axis=0)
    biases_grad = jnp.stack([bias_one, bias_two], axis=0)
    return (
        head_output,
        images_grad.reshape(image_count, grid_side, grid_side, width),
        reduce_part,
        spatial_part,
        expand_part,
        gains_grad,
        biases_grad,
        outgain_grad,
        outbias_grad,
        heads_grad,
    )


def solution(mesh):
    placed = (
        P(("dp", "task"), None, None, None),
        P(("dp", "task"), None),
        P(("dp", "task"), None, None),
        P(("dp", "task"), None, None, None),
        P(),
        P(),
        P(),
        P(),
        P(),
        P(),
        P(),
        P(None, None, "task"),
        P("dp", None, None, None, "task"),
    )
    return jax.shard_map(
        on_device,
        mesh=mesh,
        in_specs=placed,
        out_specs=(
            P("dp", None, None, None, "task"),
            P(("dp", "task"), None, None, None),
            P(("dp", "task"), None),
            P(None, ("dp", "task"), None),
            P(("dp", "task"), None),
            P(),
            P(),
            P(),
            P(),
            P("dp", None, "task"),
        ),
        check_vma=False,
    )
```

profile of v0, /device:TPU:0, one launch (start us, length us, event | category | flops | bytes accessed | tf_op | source)
XLA Modules:
  0.0 1031.1 jit_solution(16869594536490431162)
XLA Ops:
  7.2 19.5 %convert_bitcast_fusion = bf16[4,16,16,3,2048]{4,2,1,0,3:T(8,128)(2,1)} fusion(bf16[2048,3,1024]{2,0,1:T(8,128)(2,1)} %param.24, bf16[4,16,16,3,1024]{4,2,3,1,0:T(8,128)(2,1)} %param.25), kind=kOutput, calls=%fused_computation.16 | convolution fusion | flops 12891193344 | bytes 31457280 | tf_op jit(solution)/shard_map/ihwtd,ctd->ihwtc/dot_general | solution.py:152
  27.6 0.7 fusion.36
  29.6 1.9 bitcast_multiply_fusion.1
  31.5 1.4 copy-done.3
  32.9 1.3 multiply_reduce_fusion.5
  34.2 42.3 %all-reduce.14 = (f32[512]{0:T(512)S(1)}, f32[]{:T(128)}) all-reduce(f32[512]{0:T(512)S(1)} %get-tuple-element.90, f32[]{:T(128)} %get-tuple-element.66), channel_id=1, replica_groups=mesh['dp'=16,'task'=2] {'dp','task'}, use_global_device_ids=true, to_apply=%region_1.2 | all-reduce | flops 513 | bytes 4104 | tf_op jit(solution)/shard_map/psum | solution.py:50
  77.4 40.3 %psum.99 = f32[512]{0:T(512)S(1)} all-reduce(f32[512]{0:T(512)S(1)} %fusion.20), channel_id=1, replica_groups=mesh['dp'=16,'task'=2] {'dp','task'}, use_global_device_ids=true, to_apply=%region_5.6 | all-reduce | flops 512 | bytes 4096 | tf_op jit(solution)/shard_map/psum | solution.py:56
  120.2 3.0 slice-done.1
  123.2 3.6 multiply_reduce_fusion.4
  126.8 39.9 %psum.100 = f32[512]{0:T(512)S(1)} all-reduce(f32[512]{0:T(512)S(1)} %get-tuple-element.92), channel_id=1, replica_groups=mesh['dp'=16,'task'=2] {'dp','task'}, use_global_device_ids=true, to_apply=%region_7.8 | all-reduce | flops 512 | bytes 4096 | tf_op jit(solution)/shard_map/psum | solution.py:50
  167.4 1.4 fusion.21
  168.8 40.6 %psum.101 = f32[512]{0:T(512)S(1)} all-reduce(f32[512]{0:T(512)S(1)} %fusion.21), channel_id=1, replica_groups=mesh['dp'=16,'task'=2] {'dp','task'}, use_global_device_ids=true, to_apply=%region_9.10 | all-reduce | flops 512 | bytes 4096 | tf_op jit(solution)/shard_map/psum | solution.py:56
  210.0 4.7 multiply_reduce_fusion.1
  214.7 40.1 %psum.102 = f32[2048]{0:T(1024)S(1)} all-reduce(f32[2048]{0:T(1024)S(1)} %get-tuple-element.94), channel_id=1, replica_groups=mesh['dp'=16,'task'=2] {'dp','task'}, use_global_device_ids=true, to_apply=%region_11.12 | all-reduce | flops 2048 | bytes 16384 | tf_op jit(solution)/shard_map/psum | solution.py:50
  255.4 2.8 fusion.16
  258.3 40.1 %psum.103 = f32[2048]{0:T(1024)S(1)} all-reduce(f32[2048]{0:T(1024)S(1)} %fusion.16), channel_id=1, replica_groups=mesh['dp'=16,'task'=2] {'dp','task'}, use_global_device_ids=true, to_apply=%region_13.14 | all-reduce | flops 2048 | bytes 16384 | tf_op jit(solution)/shard_map/psum | solution.py:56
  299.0 10.5 %fusion.7 = (f32[2,16,16,2048]{3,2,1,0:T(8,128)S(1)}, f32[2,16,16,2048]{3,2,1,0:T(8,128)S(1)}) fusion(bf16[4,16,16,3,2048]{4,2,1,0,3:T(8,128)(2,1)} %all-reduce.17.cloned.1.call-done, u32[]{:T(128)S(6)} %multiply.10), kind=kLoop, calls=%fused_computation.13 | loop fusion | flops 13631488 | bytes 14680068 | tf_op jit(solution)/shard_map/reduce_sum | solution.py:170
  309.5 3.7 subtract_multiply_fusion
  313.3 8.9 fusion.10
  322.3 5.4 fusion.28
  327.7 40.3 %all-reduce.13 = (f32[2048]{0:T(1024)S(1)}, f32[2048]{0:T(1024)S(1)}) all-reduce(f32[2048]{0:T(1024)S(1)} %get-tuple-element.43, f32[2048]{0:T(1024)S(1)} %get-tuple-element.42), channel_id=1, replica_groups=mesh['dp'=16,'task'=2] {'dp','task'}, use_global_device_ids=true, to_apply=%region_21.22 | all-reduce | flops 4096 | bytes 32768 | tf_op jit(solution)/shard_map/psum | solution.py:63
  368.0 5.6 multiply_convert_fusion
  373.6 1.3 copy-done.15
  374.9 3.5 fusion.26
  378.4 4.6 fusion.30
  383.0 41.1 %all-reduce.12 = (f32[512]{0:T(512)S(1)}, f32[512]{0:T(512)S(1)}) all-reduce(f32[512]{0:T(512)S(1)} %get-tuple-element.47, f32[512]{0:T(512)S(1)} %get-tuple-element.46), channel_id=1, replica_groups=mesh['dp'=16,'task'=2] {'dp','task'}, use_global_device_ids=true, to_apply=%region_25.26 | all-reduce | flops 1024 | bytes 8192 | tf_op jit(solution)/shard_map/psum | solution.py:63
  424.1 2.5 multiply_convert_fusion.3
  426.6 4.9 fusion.14
  431.5 3.1 slice_bitcast_fusion.8
  435.2 0.7 copy-done.12
  436.6 1.3 pad_add_fusion.1
  437.9 1.6 fusion.29
  439.5 40.4 %all-reduce.11 = (f32[512]{0:T(512)S(1)}, f32[512]{0:T(512)S(1)}) all-reduce(f32[512]{0:T(512)S(1)} %get-tuple-element.45, f32[512]{0:T(512)S(1)} %get-tuple-element.44), channel_id=1, replica_groups=mesh['dp'=16,'task'=2] {'dp','task'}, use_global_device_ids=true, to_apply=%region_29.30 | all-reduce | flops 1024 | bytes 8192 | tf_op jit(solution)/shard_map/psum | solution.py:63
  479.8 2.2 multiply_convert_fusion.2
  482.0 0.8 copy-done.9
  482.8 3.3 fusion.39
  486.2 16.7 %bitcast_convert_fusion = bf16[2048,3,1024]{2,0,1:T(8,128)(2,1)S(1)} fusion(bf16[4,16,16,3,1024]{4,2,3,1,0:T(8,128)(2,1)} %param.25, bf16[4,16,16,2048]{3,2,1,0:T(8,128)(2,1)} %all-gather.2.cloned.1.call-done), kind=kOutput, calls=%fused_computation | convolution fusion | flops 12891193344 | bytes 23068672 | tf_op jit(solution)/shard_map/pc,ptd->ctd/dot_general | solution.py:163
  502.8 5.2 copy.58
  508.0 5.3 all-to-all-start
  513.4 6.9 copy.56
  520.4 7.5 fusion.23
  529.2 6.3 multiply_add_fusion
  535.4 15.8 %convolution_convert_fusion = bf16[1024,3,1024]{2,0,1:T(8,128)(2,1)S(1)} fusion(bf16[1024,2048,1]{1,0,2:T(8,128)(2,1)S(1)} %bitcast.177, bf16[2048,3,1024]{2,0,1:T(8,128)(2,1)} %param.24), kind=kOutput, calls=%fused_computation.35 | convolution fusion | flops 12888047616 | bytes 23068672 | tf_op jit(solution)/shard_map/pc,ctd->ptd/dot_general | solution.py:144
  551.2 3.4 copy.59
  554.7 212.7 %all-to-all-done = bf16[16,128,3,1024]{3,1,2,0:T(8,128)(2,1)} async-done(((bf16[16,128,3,1024]{3,1,2,0:T(8,128)(2,1)}), bf16[16,128,3,1024]{3,1,2,0:T(8,128)(2,1)}, u32[]{:S(2)}, u32[]{:S(2)}) %all-to-all-start) | async-done | bytes 12582944 | tf_op jit(solution)/shard_map/all_to_all | solution.py:19
  767.4 9.0 convert_reduce_fusion
  776.4 89.2 %reduce-scatter.7.cloned.1.call-done = f32[64,512]{1,0:T(8,128)} async-done(((f32[2048,512]{1,0:T(8,128)}), f32[64,512]{1,0:T(8,128)}) %reduce-scatter.7.cloned.1.call-update) | async-done | bytes 131088 | tf_op jit(solution)/shard_map/reduce_scatter | solution.py:205
  865.6 158.5 %reduce-scatter.9.cloned.1.call-done = f32[9,16,512]{2,1,0:T(8,128)} async-done(((f32[9,512,512]{2,1,0:T(8,128)}), f32[9,16,512]{2,1,0:T(8,128)}) %reduce-scatter.9.cloned.1.call-update) | async-done | bytes 294928 | tf_op jit(solution)/shard_map/reduce_scatter | solution.py:206
  (113 shorter events, 10.1 us)
Async XLA Ops:
  7.2 202.8 %copy-start = (bf16[512,2048]{1,0:T(8,128)(2,1)S(1)}, bf16[512,2048]{1,0:T(8,128)(2,1)}, u32[]{:S(2)}) copy-start(bf16[512,2048]{1,0:T(8,128)(2,1)} %param.19) | copy-start | bytes 6291460
  7.2 291.8 %all-reduce.17.cloned.1.call-start = ((), (), s32[]{:S(2)}) async-start(), calls=%async_computation.8 | async-start | bytes 25165824
  26.7 0.7 copy-start.32
  26.7 0.9 copy-start.20
  26.7 1.6 copy-start.36
  26.7 459.4 %all-gather.2.cloned.1.call-start = ((), (), s32[]{:S(2)}) async-start(), calls=%async_computation.4 | async-start | bytes 6291456 | tf_op jit(solution)/shard_map/all_gather | solution.py:138
  28.3 451.5 %copy-start.17 = (f32[512]{0:T(512)}, f32[512]{0:T(512)S(1)}, u32[]{:S(2)}) copy-start(f32[512]{0:T(512)S(1)} %mul.306) | copy-start | bytes 6148
  29.6 3.4 copy-start.16
  31.5 1.4 copy-start.3
  32.9 84.8 %copy-start.33 = (f32[2,512]{1,0:T(2,128)S(1)}, f32[2,512]{1,0:T(2,128)}, u32[]{:S(2)}) copy-start(f32[2,512]{1,0:T(2,128)} %param.20) | copy-start | bytes 12292
  32.9 84.8 %copy-start.34 = (f32[2,512]{1,0:T(2,128)S(1)}, f32[2,512]{1,0:T(2,128)}, u32[]{:S(2)}) copy-start(f32[2,512]{1,0:T(2,128)} %param.21) | copy-start | bytes 12292
  118.8 1.4 slice-start
  119.5 3.7 slice-start.1
  120.2 6.6 copy-start.6
  214.7 83.6 %copy-start.19 = (f32[2048]{0:T(1024)S(1)}, f32[2048]{0:T(1024)}, u32[]{:S(2)}) copy-start(f32[2048]{0:T(1024)} %param.22) | copy-start | bytes 24580
  313.2 9.0 copy-start.2
  313.2 9.0 copy-start.5
  313.3 9.0 copy-start.21
  327.6 448.8 %reduce-scatter.11.cloned.1.call-start = ((), (), s32[]{:S(2)}) async-start(), calls=%async_computation.7 | async-start | bytes 4325376 | tf_op jit(solution)/shard_map/reduce_scatter | solution.py:207
  368.0 5.6 copy-start.22
  368.0 5.6 copy-start.23
  368.0 6.9 copy-start.11
  373.6 1.3 copy-start.15
  378.4 487.2 %reduce-scatter.7.cloned.1.call-start = ((), (), s32[]{:S(2)}) async-start(), calls=%async_computation.5 | async-start | bytes 4325376 | tf_op jit(solution)/shard_map/reduce_scatter | solution.py:205
  424.1 7.4 copy-start.24
  424.1 7.4 copy-start.26
  426.6 4.9 copy-start.7
  434.7 1.2 copy-start.12
  434.7 1.6 copy-start.13
  434.7 1.9 copy-start.14
  437.9 45.0 %copy-start.4 = (bf16[512,2048]{1,0:T(8,128)(2,1)S(1)}, bf16[512,2048]{1,0:T(8,128)(2,1)}, u32[]{:S(2)}) copy-start(bf16[512,2048]{1,0:T(8,128)(2,1)} %copy-done.3) | copy-start | bytes 6291460
  479.8 6.3 copy-start.28
  479.8 6.3 copy-start.30
  482.0 0.8 copy-start.9
  508.0 259.4 %all-to-all-start = ((bf16[16,128,3,1024]{3,1,2,0:T(8,128)(2,1)}), bf16[16,128,3,1024]{3,1,2,0:T(8,128)(2,1)}, u32[]{:S(2)}, u32[]{:S(2)}) async-start(bf16[16,128,3,1024]{3,1,2,0:T(8,128)(2,1)} %copy.58), calls=%async_computation.3 | async-start | bytes 25165824 | tf_op jit(solution)/shard_map/all_to_all | solution.py:19
  513.4 510.7 %reduce-scatter.9.cloned.1.call-start = ((), (), s32[]{:S(2)}) async-start(), calls=%async_computation.6 | async-start | bytes 9732096 | tf_op jit(solution)/shard_map/reduce_scatter | solution.py:206
  513.4 7.0 copy-start.8
  527.8 0.7 copy-start.25
  527.8 0.7 copy-start.27
  527.8 0.7 copy-start.29
  527.8 0.7 copy-start.31
  527.8 1.3 copy-start.10
  527.9 1.3 copy-start.18
  529.2 6.3 copy-start.35
  551.2 472.9 %copy-start.1 = (bf16[512,2048]{1,0:T(8,128)(2,1)S(1)}, bf16[512,2048]{1,0:T(8,128)(2,1)}, u32[]{:S(2)}) copy-start(bf16[512,2048]{1,0:T(8,128)(2,1)} %param.19) | copy-start | bytes 6291460
Sparse Core Ops, SparseCore 0:
  26.8 52.2 all-reduce.16
  327.8 14.4 all-gather.1
  378.5 142.5 reduce-scatter.10
  523.8 341.7 reduce-scatter.6
  868.3 155.7 reduce-scatter.8
where the time goes:
time: 1040 us; the launch traced here: 1030 us
  waiting for transfers between devices  461 us (44%)
  blocking collectives  365 us (35%)
  matrix products  91.3 us (9%)
  other arithmetic  63.5 us (6%)
  local copies, waits for them, and re-layouts  29.8 us (3%)
  between operations  15.5 us (1%)
    all_to_all x1, waiting for transfers between devices, sent_and_summed(): tiles = lax.all_to_all(cut_along(value, dim, peers), axis, 0, 0, tiled=True)  213 us
    reduce_scatter x1, waiting for transfers between devices, on_device(): lax.psum_scatter(spatial_part, ('dp', 'task'), scatter_dimension=1, tiled...  159 us
    psum x3, blocking collectives, moments(): lax.psum((jnp.sum(valid_cells * values, axis=0), jnp.sum(valid_cells)), (...  122 us
    psum x3, blocking collectives, norm_back(): lax.psum((jnp.sum(grad_shifted, axis=0), jnp.sum(grad_shifted * normed, a...  122 us
    psum x3, blocking collectives, moments(): lax.psum(jnp.sum(valid_cells * deviation * deviation, axis=0), ('dp', 'ta...  121 us
    reduce_scatter x1, waiting for transfers between devices, on_device(): lax.psum_scatter(reduce_part, ('dp', 'task'), scatter_dimension=0, tiled=...  89.2 us
  transfers between devices with their start and end apart: 6, of which 3 were waited for; matrix products, arithmetic and copies ran while one was open for 12% of the time, Pallas kernels for 0%

commit v1 on v0

v1 whole, which is shorter than its diff:
```python
import jax
import jax.numpy as jnp
from jax import lax
from jax.sharding import PartitionSpec as P

epsilon = 1e-05
steepness = 6.0
levels = 4096.0
everyone = ("dp", "task")


def validity(bucket_shape, pixel_mask):
    row_index = lax.broadcasted_iota(jnp.int32, pixel_mask.shape, 1)
    col_index = lax.broadcasted_iota(jnp.int32, pixel_mask.shape, 2)
    inside = (row_index < bucket_shape[:, 0][:, None, None]) & (
        col_index < bucket_shape[:, 1][:, None, None]
    )
    return jnp.where(inside, pixel_mask, 0).astype(jnp.float32)


def inner_rows(left, right):
    return lax.dot_general(
        left, right, (((0,), (0,)), ((), ())), preferred_element_type=jnp.float32
    )


def outer_back(left, right):
    return lax.dot_general(
        left, right, (((1,), (1,)), ((), ())), preferred_element_type=jnp.float32
    )


def silu_slope(values):
    sigma = jax.nn.sigmoid(values)
    return sigma * (1.0 + values * (1.0 - sigma))


def from_everyone(rows):
    count = lax.axis_size("dp") * lax.axis_size("task")
    k, channels = rows.shape
    sent = jnp.broadcast_to(rows.reshape(1, k * channels // 128, 128), (count, k * channels // 128, 128))
    return lax.all_to_all(sent, everyone, 0, 0, tiled=True).reshape(count, k, channels)


def moments(values, valid_cells, local_count, counts):
    channels = values.shape[1]
    first = jnp.sum(valid_cells * values, axis=0)
    local_center = first / jnp.maximum(local_count, 1.0)
    deviation = values - local_center
    second = jnp.sum(valid_cells * deviation * deviation, axis=0)
    rows = [first, second]
    if counts is None:
        rows.append(jnp.full((channels,), local_count))
    table = from_everyone(jnp.stack(rows))
    if counts is None:
        counts = table[:, 2, 0]
    valid_count = jnp.sum(counts)
    center = jnp.sum(table[:, 0], axis=0) / valid_count
    shift = table[:, 0] / jnp.maximum(counts, 1.0)[:, None] - center
    variance = (
        jnp.sum(table[:, 1], axis=0) + jnp.sum(counts[:, None] * shift * shift, axis=0)
    ) / valid_count
    inverse_std = lax.rsqrt(variance + epsilon)
    return (values - center) * inverse_std, inverse_std, counts, valid_count


def norm_back(grad_shifted, normed, inverse_std, gain, valid_cells, valid_count):
    rows = jnp.stack([jnp.sum(grad_shifted, axis=0), jnp.sum(grad_shifted * normed, axis=0)])
    totals = jnp.sum(from_everyone(rows), axis=0)
    bias_grad, gain_grad = totals[0], totals[1]
    grad_values = (
        gain
        * inverse_std
        * (grad_shifted - valid_cells * (bias_grad + normed * gain_grad) / valid_count)
    )
    return (grad_values.astype(jnp.bfloat16), gain_grad, bias_grad)


def patches(acts):
    grid_side = acts.shape[1]
    padded = jnp.pad(acts, ((0, 0), (1, 1), (1, 1), (0, 0)))
    windows = []
    for offset in range(9):
        row_shift = offset // 3
        col_shift = offset % 3
        windows.append(
            padded[:, row_shift : row_shift + grid_side, col_shift : col_shift + grid_side, :]
        )
    return jnp.concatenate(windows, axis=-1).reshape(-1, 9 * acts.shape[-1])


def unpatch(grad_cols, image_count, grid_side, channels):
    blocks = grad_cols.reshape(image_count, grid_side, grid_side, 9, channels)
    result = jnp.zeros((image_count, grid_side + 2, grid_side + 2, channels), jnp.float32)
    for offset in range(9):
        row_shift = offset // 3
        col_shift = offset % 3
        result = result + jnp.pad(
            blocks[:, :, :, offset, :],
            ((0, 0), (row_shift, 2 - row_shift), (col_shift, 2 - col_shift), (0, 0)),
        )
    return result[:, 1 : grid_side + 1, 1 : grid_side + 1, :]


def dp_bit(bit):
    return (lax.axis_index("dp") >> bit) & 1


def swap_dp(value, bit):
    peers = lax.axis_size("dp")
    return lax.ppermute(value, "dp", [(i, i ^ (1 << bit)) for i in range(peers)])


def swap_core(value):
    return lax.ppermute(value, "task", [(0, 1), (1, 0)])


def pick(value, axis, index):
    return lax.dynamic_index_in_dim(value, index, axis, keepdims=False)


def halve(value, dims, order):
    dims = list(dims)
    for bit in order:
        axis = dims.index(bit)
        mine = dp_bit(bit)
        arrived = swap_dp(pick(value, axis, 1 - mine), bit)
        kept = pick(value, axis, mine).astype(jnp.float32)
        dims.pop(axis)
        total = kept + arrived.astype(jnp.float32)
        value = total.astype(jnp.bfloat16) if dims else total
    return value


def on_device(
    images,
    bucket_shape,
    pixel_mask,
    thresholds,
    reduce_weight,
    spatial_weight,
    expand_weight,
    mid_gains,
    mid_biases,
    out_gain,
    out_bias,
    head_weights,
    head_cotangent,
):
    image_count = images.shape[0]
    grid_side = images.shape[1]
    width = images.shape[3]
    middle = reduce_weight.shape[1]
    head_count = head_weights.shape[1]
    pixels = image_count * grid_side * grid_side
    peers = lax.axis_size("dp")
    bits = peers.bit_length() - 1
    core = lax.axis_index("task")
    valid_cells = validity(bucket_shape, pixel_mask).reshape(pixels, 1)
    local_count = jnp.sum(valid_cells)
    inputs = images.reshape(pixels, width)
    masked = inputs * valid_cells.astype(jnp.bfloat16)

    group_images = head_cotangent.shape[0]
    task_part = jnp.einsum(
        "ihwtd,ctd->ihwtc", head_cotangent, head_weights, preferred_element_type=jnp.float32
    ).reshape(2, pixels, head_count, width)
    task_sent = pick(task_part, 0, 1 - core).astype(jnp.bfloat16)
    task_kept = pick(task_part, 0, core).astype(jnp.bfloat16).astype(jnp.float32)
    task_grad = task_kept + swap_core(task_sent).astype(jnp.float32)
    task_total = jnp.sum(task_grad, axis=1)
    spread = jnp.sum(jnp.sqrt(task_grad * task_grad + 1.0), axis=1)
    purity = 0.5 * (1.0 + task_total / spread)
    threshold_level = (thresholds.reshape(pixels, width).astype(jnp.float32) + 0.5) / levels
    kept_share = jax.nn.sigmoid(
        steepness * jnp.tanh(task_grad) * (purity - threshold_level)[:, None, :]
    )
    merged = jnp.sum(kept_share * task_grad, axis=1)

    pre_reduce = jnp.dot(masked, reduce_weight, preferred_element_type=jnp.float32)
    normed_reduce, inverse_reduce, counts, valid_count = moments(
        pre_reduce, valid_cells, local_count, None
    )
    shifted_reduce = mid_gains[0] * normed_reduce + mid_biases[0]
    act_reduce = (valid_cells * jax.nn.silu(shifted_reduce)).astype(jnp.bfloat16)
    patches_flat = patches(act_reduce.reshape(image_count, grid_side, grid_side, middle))
    spatial_flat = spatial_weight.reshape(9 * middle, middle)
    pre_spatial = jnp.dot(patches_flat, spatial_flat, preferred_element_type=jnp.float32)
    normed_spatial, inverse_spatial, _, _ = moments(pre_spatial, valid_cells, local_count, counts)
    shifted_spatial = mid_gains[1] * normed_spatial + mid_biases[1]
    act_spatial = (valid_cells * jax.nn.silu(shifted_spatial)).astype(jnp.bfloat16)
    pre_expand = jnp.dot(act_spatial, expand_weight, preferred_element_type=jnp.float32)
    normed_expand, inverse_expand, _, _ = moments(pre_expand, valid_cells, local_count, counts)
    residual = inputs.astype(jnp.float32) + out_gain * normed_expand + out_bias
    features = (valid_cells * jax.nn.silu(residual)).astype(jnp.bfloat16)
    gathered = lax.all_gather(features, "task", axis=0, tiled=True)

    lanes = head_weights.shape[2]
    orders = ([0, 1] + list(range(2, bits)), [1, 0] + list(range(2, bits)))
    cut = gathered.reshape((gathered.shape[0],) + (2,) * bits + (width // peers,))
    dims = list(range(bits - 1, -1, -1))
    flat_cotangent = head_cotangent.reshape(gathered.shape[0], head_count, lanes)
    heads_parts = []
    for part, order in enumerate(orders):
        part_cot = flat_cotangent[:, :, part * lanes // 2 : (part + 1) * lanes // 2]
        axis = dims.index(order[0])
        mine = dp_bit(order[0])

        def product(index):
            chosen = pick(cut, 1 + axis, index).reshape(gathered.shape[0], width // 2)
            return jnp.einsum("pc,ptd->tcd", chosen, part_cot, preferred_element_type=jnp.float32)

        arrived = swap_dp(product(1 - mine).astype(jnp.bfloat16), order[0])
        kept = (product(mine) + arrived.astype(jnp.float32)).astype(jnp.bfloat16)
        rest = [d for d in dims if d != order[0]]
        kept = kept.reshape((head_count,) + (2,) * (bits - 1) + (width // peers, lanes // 2))
        kept = jnp.moveaxis(kept, 0, bits - 1)
        heads_parts.append(halve(kept, rest, order[1:]))
    heads_grad = jnp.concatenate(heads_parts, axis=-1)
    heads_grad = jnp.moveaxis(heads_grad, 0, 1)

    head_values = jnp.einsum(
        "pc,ctd->ptd", gathered, head_weights, preferred_element_type=jnp.float32
    )
    head_output = head_values.astype(jnp.bfloat16).reshape(
        group_images, grid_side, grid_side, head_count, -1
    )

    grad_residual = merged * valid_cells * silu_slope(residual)
    grad_expand, outgain_grad, outbias_grad = norm_back(
        grad_residual, normed_expand, inverse_expand, out_gain, valid_cells, valid_count
    )
    expand_part = inner_rows(act_spatial, grad_expand)
    grad_act_spatial = outer_back(grad_expand, expand_weight)
    grad_spatial, gain_two, bias_two = norm_back(
        grad_act_spatial * valid_cells * silu_slope(shifted_spatial),
        normed_spatial,
        inverse_spatial,
        mid_gains[1],
        valid_cells,
        valid_count,
    )
    spatial_part = inner_rows(patches_flat, grad_spatial).reshape(9, middle, middle)
    grad_cols = outer_back(grad_spatial, spatial_flat)
    grad_act_reduce = unpatch(grad_cols, image_count, grid_side, middle).reshape(pixels, middle)
    grad_reduce, gain_one, bias_one = norm_back(
        grad_act_reduce * valid_cells * silu_slope(shifted_reduce),
        normed_reduce,
        inverse_reduce,
        mid_gains[0],
        valid_cells,
        valid_count,
    )
    reduce_part = inner_rows(masked, grad_reduce)
    images_grad = grad_residual + valid_cells * outer_back(grad_reduce, reduce_weight)

    devices = peers * 2
    def by_device(value):
        return value.reshape((2,) * bits + (2,) + value.shape[1:])
    def shared(value, order):
        axis = bits
        arrived = swap_core(pick(value, axis, 1 - core).astype(jnp.bfloat16))
        total = pick(value, axis, core) + arrived.astype(jnp.float32)
        return halve(total.astype(jnp.bfloat16), dims, order)
    expand_rows = middle // devices
    expand_cut = jnp.moveaxis(
        expand_part.reshape(devices, expand_rows, width // middle, middle), 2, 1
    ).reshape(devices, expand_rows * width // middle, middle)
    spatial_cut = jnp.moveaxis(
        spatial_part.reshape(9, devices, middle // devices, middle), 1, 0
    ).reshape(devices, 9 * (middle // devices), middle)
    early = shared(by_device(jnp.concatenate([expand_cut, spatial_cut], axis=1)), orders[0])
    late = shared(by_device(reduce_part.reshape(devices, width // devices, middle)), orders[1])
    split = expand_rows * width // middle
    expand_grad = jnp.moveaxis(
        early[:split].reshape(width // middle, expand_rows, middle), 0, 1
    ).reshape(expand_rows, width)
    spatial_grad = early[split:].reshape(9, middle // devices, middle)
    reduce_grad = late
    gains_grad = jnp.stack([gain_one, gain_two], axis=0)
    biases_grad = jnp.stack([bias_one, bias_two], axis=0)
    return (
        head_output,
        images_grad.reshape(image_count, grid_side, grid_side, width),
        reduce_grad,
        spatial_grad,
        expand_grad,
        gains_grad,
        biases_grad,
        outgain_grad,
        outbias_grad,
        heads_grad,
    )


def solution(mesh):
    placed = (
        P(("dp", "task"), None, None, None),
        P(("dp", "task"), None),
        P(("dp", "task"), None, None),
        P(("dp", "task"), None, None, None),
        P(),
        P(),
        P(),
        P(),
        P(),
        P(),
        P(),
        P(None, None, "task"),
        P("dp", None, None, None, "task"),
    )
    return jax.shard_map(
        on_device,
        mesh=mesh,
        in_specs=placed,
        out_specs=(
            P("dp", None, None, None, "task"),
            P(("dp", "task"), None, None, None),
            P(("dp", "task"), None),
            P(None, ("dp", "task"), None),
            P(("dp", "task"), None),
            P(),
            P(),
            P(),
            P(),
            P("dp", None, "task"),
        ),
        check_vma=False,
    )
```

time: 1040 us -> 564 us (0.54)
  blocking collectives: 365 us -> 13.8 us
  waiting for transfers between devices: 461 us -> 165 us
  local copies, waits for them, and re-layouts: 29.8 us -> 132 us
  starting transfers between devices: 5.51 us -> 42.5 us
  other arithmetic: 63.5 us -> 97 us
    psum x9 -> x0, blocking collectives: 365 us -> none  [the longest x3 122 us: moments(): lax.psum((jnp.sum(valid_cells * values, axis=0), jnp.sum(valid_cells)), (...]
    reduce_scatter x3 -> x0, waiting for transfers between devices: 248 us -> none  [the longest x1 159 us: on_device(): lax.psum_scatter(spatial_part, ('dp', 'task'), scatter_dimension=1, tiled...]
    all_to_all x1 -> x5, waiting for transfers between devices: 213 us -> 15.4 us  [from_everyone(): lax.all_to_all(sent, everyone, 0, 0, tiled=True).reshape(count, k, channels)]
    ppermute x0 -> x19, waiting for transfers between devices: none -> 150 us  [the longest x16 150 us: swap_dp(): return lax.ppermute(value, 'dp', [(i, i ^ 1 << bit) for i in range(peers)])]
    dynamic_slice x0 -> x8, local copies, waits for them, and re-layouts: none -> 46.9 us  [pick(): return lax.dynamic_index_in_dim(value, index, axis, keepdims=False)]
    ppermute x0 -> x19, starting transfers between devices: none -> 19.5 us  [the longest x16 18.6 us: swap_dp(): return lax.ppermute(value, 'dp', [(i, i ^ 1 << bit) for i in range(peers)])]
    reshape x1 -> x7, local copies, waits for them, and re-layouts: 5.21 us -> 23.3 us  [the longest x2 12 us: on_device(): expand_part.reshape(devices, expand_rows, width // middle, middle)]
    all_to_all x1 -> x5, starting transfers between devices: 5.31 us -> 23 us  [from_everyone(): lax.all_to_all(sent, everyone, 0, 0, tiled=True).reshape(count, k, channels)]
  transfers between devices with their start and end apart: 6 -> 25, of which waited for: 3 -> 9; matrix products, arithmetic and copies ran while one was open for 12% -> 45% of each run, Pallas kernels for 0% -> 0%
where the time goes in v1:
time: 564 us; the launch traced here: 558 us
  waiting for transfers between devices  165 us (29%)
  local copies, waits for them, and re-layouts  132 us (23%)
  other arithmetic  97 us (17%)
  matrix products  91.8 us (16%)
  starting transfers between devices  42.5 us (8%)
  between operations  16 us (3%)
  blocking collectives  13.8 us (2%)
    ppermute x16, waiting for transfers between devices, swap_dp(): return lax.ppermute(value, 'dp', [(i, i ^ 1 << bit) for i in range(peers)])  150 us
    dynamic_slice x8, local copies, waits for them, and re-layouts, pick(): return lax.dynamic_index_in_dim(value, index, axis, keepdims=False)  46.9 us
    unnamed x91, local copies, waits for them, and re-layouts  26.8 us
    dot_general x4, matrix products, product(): jnp.einsum('pc,ptd->tcd', chosen, part_cot, preferred_element_type=jnp.fl...  25 us
    all_to_all x5, starting transfers between devices, from_everyone(): lax.all_to_all(sent, everyone, 0, 0, tiled=True).reshape(count, k, channels)  23 us
    dot_general x1, matrix products, on_device(): jnp.einsum('ihwtd,ctd->ihwtc', head_cotangent, head_weights, preferred_el...  19.3 us
    ppermute x16, starting transfers between devices, swap_dp(): return lax.ppermute(value, 'dp', [(i, i ^ 1 << bit) for i in range(peers)])  18.6 us
    reduce_sum x1, other arithmetic, on_device(): spread = jnp.sum(jnp.sqrt(task_grad * task_grad + 1.0), axis=1)  16.4 us
  transfers between devices with their start and end apart: 25, of which 9 were waited for; matrix products, arithmetic and copies ran while one was open for 45% of the time, Pallas kernels for 0%

profile of v1, /device:TPU:0, one launch (start us, length us, event | category | flops | bytes accessed | tf_op | source)
XLA Modules:
  0.0 557.7 jit_solution(3346788979879608064)
XLA Ops:
  16.7 7.3 %all-to-all-start = ((f32[32,12,128]{2,1,0:T(8,128)}), f32[32,12,128]{2,1,0:T(8,128)S(1)}, u32[]{:S(2)}, u32[]{:S(2)}) async-start(f32[32,12,128]{2,1,0:T(8,128)} %broadcast_in_dim.30), calls=%async_computation | async-start | bytes 524288 | tf_op jit(solution)/shard_map/all_to_all | solution.py:42
  24.0 19.3 %fusion = bf16[3,2048,4,16,16]{1,4,3,2,0:T(8,128)(2,1)} fusion(bf16[2048,3,1024]{2,0,1:T(8,128)(2,1)} %param.24, bf16[4,16,16,3,1024]{4,2,3,1,0:T(8,128)(2,1)} %param.25), kind=kOutput, calls=%fused_computation.6 | convolution fusion | flops 12884901888 | bytes 31457280 | tf_op jit(solution)/shard_map/ihwtd,ctd->ihwtc/dot_general | solution.py:165
  43.3 6.6 %fusion.9 = bf16[512,3,2048]{2,0,1:T(8,128)(2,1)} fusion(bf16[2,512,3,2048]{3,1,0,2:T(8,128)(2,1)} %bitcast.328, s32[]{:T(128)S(6)} %select_n.80), kind=kLoop, calls=%fused_computation.18 | loop fusion | bytes 12582916 | tf_op jit(solution)/shard_map/convert_element_type | solution.py:168
  57.2 3.0 slice-done.3
  64.0 13.8 %all_to_all.30 = f32[32,8,128]{2,1,0:T(8,128)S(1)} all-to-all(f32[32,8,128]{2,1,0:T(8,128)S(1)} %broadcast_in_dim.32), channel_id=1, replica_groups=mesh['dp'=16,'task'=2] {'dp','task'}, dimensions={0} | all-to-all | bytes 262144 | tf_op jit(solution)/shard_map/all_to_all | solution.py:42
  85.7 3.6 all-to-all-start.2
  89.3 5.0 add_multiply_fusion
  94.3 10.5 %all-to-all-done.2 = f32[32,32,128]{2,1,0:T(8,128)} async-done(((f32[32,32,128]{2,1,0:T(8,128)}), f32[32,32,128]{2,1,0:T(8,128)}, u32[]{:S(2)}, u32[]{:S(2)}) %all-to-all-start.2) | async-done | bytes 524320 | tf_op jit(solution)/shard_map/all_to_all | solution.py:42
  110.2 16.4 %sqrt_reduce_fusion = (f32[512,2048]{1,0:T(8,128)S(1)}, f32[512,2048]{1,0:T(8,128)}, bf16[512,3,2048]{2,0,1:T(8,128)(2,1)S(1)}) fusion(bf16[512,3,2048]{2,0,1:T(8,128)(2,1)} %collective-permute-done, bf16[2,512,3,2048]{3,1,0,2:T(8,128)(2,1)} %bitcast.329, s32[]{:T(128)S(6)} %select_n.79), kind=kLoop, calls=%fused_computation.9 | loop fusion | flops 19922944 | bytes 27262980 | tf_op jit(solution)/shard_map/reduce_sum | solution.py:172
  126.7 3.8 fusion.16
  130.5 9.3 %multiply_reduce_fusion = f32[512,2048]{1,0:T(8,128)S(1)} fusion(bf16[512,3,2048]{2,0,1:T(8,128)(2,1)} %collective-permute-done, bf16[512,3,2048]{2,0,1:T(8,128)(2,1)S(1)} %get-tuple-element.112, f32[512,2048]{1,0:T(8,128)S(1)} %fusion.16), kind=kLoop, calls=%fused_computation.8 | loop fusion | flops 27262976 | bytes 20971520 | tf_op jit(solution)/shard_map/reduce_sum | solution.py:178
  139.8 14.6 %fusion.69 = (f32[2048]{0:T(1024)S(1)}, f32[2048]{0:T(1024)S(1)}, f32[512,2048]{1,0:T(8,128)}, bf16[512,2048]{1,0:T(8,128)(2,1)}) fusion(f32[2048]{0:T(1024)S(1)} %get-tuple-element.110, f32[512,2048]{1,0:T(8,128)S(1)} %copy-done.6, f32[2048]{0:T(1024)S(1)} %broadcast_divide_fusion, f32[2048]{0:T(1024)S(1)} %copy-done.34, f32[2048]{0:T(1024)S(1)} %copy-done.30, ...), kind=kLoop, calls=%fused_computation.221 | loop fusion | flops 22016000 | bytes 16828416 | tf_op jit(solution)/shard_map/reduce_sum | solution.py:68
  155.3 3.3 all-to-all-start.3
  158.7 3.9 copy.211
  162.7 6.6 %copy.213 = bf16[4608,512]{1,0:T(8,128)(2,1)} copy(bf16[4608,512]{0,1:T(8,128)(2,1)} %bitcast.339) | data formatting | bytes 9437184 | tf_op jit(solution)/shard_map/dot_general | solution.py:22
  169.3 4.9 all-to-all-done.3
  175.3 6.7 %multiply_convert_fusion = bf16[512,2048]{1,0:T(8,128)(2,1)S(1)} fusion(f32[512,2048]{1,0:T(8,128)} %get-tuple-element.111, f32[512,2048]{1,0:T(8,128)} %copy-done.5, f32[]{:T(128)} %get-tuple-element.101, f32[2048]{0:T(1024)S(1)} %get-tuple-element.145, f32[2048]{0:T(1024)S(1)} %get-tuple-element.144, f32[2048]{0:T(1024)S(1)} %get-tuple-element.109, ...), kind=kLoop, calls=%fused_computation.33 | loop fusion | flops 9437184 | bytes 10528772 | tf_op jit(solution)/shard_map/convert_element_type | solution.py:76
  188.1 5.4 fusion.67
  193.5 6.0 %reshape.313 = f32[32,16,4,512]{3,2,1,0:T(4,128)} reshape(f32[512,2048]{1,0:T(8,128)} %fusion.67) | data formatting | bytes 8388608 | tf_op jit(solution)/shard_map/reshape | solution.py:267
  199.5 6.0 %copy.212 = f32[32,16,4,512]{3,1,2,0:T(8,128)} copy(f32[32,16,4,512]{3,2,1,0:T(4,128)} %reshape.313) | data formatting | bytes 8388608 | tf_op jit(solution)/shard_map/reshape | solution.py:267
  207.8 4.7 fusion.13
  212.4 3.1 slice_bitcast_fusion.8
  220.7 6.2 %all-to-all-start.5 = ((f32[32,8,128]{2,1,0:T(8,128)}), f32[32,8,128]{2,1,0:T(8,128)S(1)}, u32[]{:S(2)}, u32[]{:S(2)}) async-start(f32[32,8,128]{2,1,0:T(8,128)} %broadcast_in_dim.40), calls=%async_computation.5 | async-start | bytes 262144 | tf_op jit(solution)/shard_map/all_to_all | solution.py:42
  226.9 7.5 %convolution_bitcast_fusion = f32[32,9,16,512]{3,2,0,1:T(8,128)} fusion(bf16[9,32,16,512]{3,2,1,0:T(8,128)(2,1)} %bitcast.327, bf16[512,512]{1,0:T(8,128)(2,1)S(1)} %multiply_convert_fusion.3), kind=kOutput, calls=%fused_computation.42 | convolution fusion | flops 2415919104 | bytes 14680064 | tf_op jit(solution)/shard_map/dot_general | solution.py:22
  234.4 5.0 copy.214
  251.3 6.9 %copy.201 = bf16[4,16,16,3,1024]{4,2,1,0,3:T(8,128)(2,1)} copy(bf16[4,16,16,3,1024]{4,2,3,1,0:T(8,128)(2,1)} %param.25) | data formatting | bytes 12582912 | tf_op args[12]
  260.2 7.7 %reshape.317 = bf16[1024,2,2,2,2,128]{5,4,3,2,1,0:T(2,128)(2,1)} reshape(bf16[1024,2048]{1,0:T(8,128)(2,1)} %all-gather.2.cloned.1.call-done) | data formatting | bytes 8388608 | tf_op jit(solution)/shard_map/reshape | solution.py:200
  267.9 11.5 %constant_dynamic-slice_fusion.7 = (bf16[1024,2,2,2,1,128]{5,4,3,2,1,0:T(2,128)(2,1)}, bf16[1024,2,2,2,1,128]{5,4,3,2,1,0:T(2,128)(2,1)}) fusion(bf16[1024,2,2,2,2,128]{5,4,3,2,1,0:T(2,128)(2,1)} %reshape.317, s32[]{:T(128)S(6)} %select_n.83, s32[]{:T(128)S(6)} %select_n.84), kind=kLoop, calls=%fused_computation.186 | loop fusion | bytes 8388616 | tf_op jit(solution)/shard_map/jit(dynamic_index_in_dim)/dynamic_slice | solution.py:119
  279.4 9.0 %copy.218 = bf16[1024,2,2,2,1,128]{0,5,3,2,1,4:T(8,128)(2,1)S(1)} copy(bf16[1024,2,2,2,1,128]{5,4,3,2,1,0:T(2,128)(2,1)} %get-tuple-element.126) | data formatting | bytes 4194304 | tf_op jit(solution)/shard_map/jit(dynamic_index_in_dim)/dynamic_slice | solution.py:119
  288.4 6.8 %convert_bitcast_fusion.1 = bf16[3,1024,512]{2,1,0:T(8,128)(2,1)} fusion(bf16[1024,1024,1]{0,1,2:T(8,128)(2,1)S(1)} %bitcast.348, bf16[1024,3,1024]{2,0,1:T(8,128)(2,1)} %bitcast.332), kind=kOutput, calls=%fused_computation.52 | convolution fusion | flops 3222798336 | bytes 8388608 | tf_op jit(solution)/shard_map/pc,ptd->tcd/dot_general | solution.py:211
  297.1 4.2 constant_dynamic-slice_fusion.3
  301.3 6.4 %copy.222 = bf16[1024,2,2,1,2,128]{0,5,4,2,1,3:T(8,128)(2,1)} copy(bf16[1024,2,2,1,2,128]{5,4,3,2,1,0:T(2,128)(2,1)} %get-tuple-element.128) | data formatting | bytes 4194304 | tf_op jit(solution)/shard_map/jit(dynamic_index_in_dim)/dynamic_slice | solution.py:119
  307.7 5.3 fusion.8
  314.6 6.8 %convert_bitcast_fusion = bf16[3,1024,512]{2,1,0:T(8,128)(2,1)} fusion(bf16[1024,1024,1]{0,1,2:T(8,128)(2,1)S(1)} %bitcast.359, bf16[1024,3,1024]{2,0,1:T(8,128)(2,1)} %bitcast.333), kind=kOutput, calls=%fused_computation.51 | convolution fusion | flops 3222798336 | bytes 8388608 | tf_op jit(solution)/shard_map/pc,ptd->tcd/dot_general | solution.py:211
  323.6 79.2 %collective-permute-done.2 = bf16[2,2,2,64,512]{4,3,2,1,0:T(8,128)(2,1)S(1)} collective-permute-done((bf16[2,2,2,64,512]{4,3,2,1,0:T(8,128)(2,1)S(1)}, bf16[2,2,2,64,512]{4,3,2,1,0:T(8,128)(2,1)S(1)}, u32[]{:S(2)}, u32[]{:S(2)}) %collective-permute-start.2) | collective-permute-done | bytes 524320 | tf_op jit(solution)/shard_map/ppermute | solution.py:111
  405.3 5.8 %collective-permute-done.3 = bf16[2,2,64,512]{3,2,1,0:T(8,128)(2,1)S(1)} collective-permute-done((bf16[2,2,64,512]{3,2,1,0:T(8,128)(2,1)S(1)}, bf16[2,2,64,512]{3,2,1,0:T(8,128)(2,1)S(1)}, u32[]{:S(2)}, u32[]{:S(2)}) %collective-permute-start.3) | collective-permute-done | bytes 262176 | tf_op jit(solution)/shard_map/ppermute | solution.py:111
  413.4 10.5 %copy.216 = bf16[1024,2,2,2,1,128]{0,5,3,2,1,4:T(8,128)(2,1)} copy(bf16[1024,2,2,2,1,128]{5,4,3,2,1,0:T(2,128)(2,1)} %get-tuple-element.125) | data formatting | bytes 4194304 | tf_op jit(solution)/shard_map/jit(dynamic_index_in_dim)/dynamic_slice | solution.py:119
  423.9 4.7 copy.221
  432.9 6.2 %fusion.12 = bf16[3,1024,512]{2,1,0:T(8,128)(2,1)S(1)} fusion(bf16[3,1024,512]{2,1,0:T(8,128)(2,1)} %collective-permute-done.11, bf16[1024,1024,1]{0,1,2:T(8,128)(2,1)S(1)} %bitcast.347, bf16[1024,3,1024]{2,0,1:T(8,128)(2,1)} %bitcast.334), kind=kOutput, calls=%fused_computation.23 | convolution fusion | flops 3225944064 | bytes 11534336 | tf_op jit(solution)/shard_map/pc,ptd->tcd/dot_general | solution.py:211
  440.7 5.2 fusion.11
  448.9 3.3 multiply_add_fusion
  455.4 2.8 collective-permute-done.5
  459.3 24.3 %collective-permute-done.12 = bf16[2,2,3,128,512]{4,3,2,0,1:T(8,128)(2,1)S(1)} collective-permute-done((bf16[2,2,3,128,512]{4,3,2,0,1:T(8,128)(2,1)S(1)}, bf16[2,2,3,128,512]{4,3,2,0,1:T(8,128)(2,1)S(1)}, u32[]{:S(2)}, u32[]{:S(2)}) %collective-permute-start.12) | collective-permute-done | bytes 1572896 | tf_op jit(solution)/shard_map/ppermute | solution.py:111
  487.0 15.9 %fusion.19 = bf16[1024,3,1024]{2,0,1:T(8,128)(2,1)S(1)} fusion(bf16[2048,3,1024]{2,0,1:T(8,128)(2,1)} %param.24, bf16[1024,2048]{1,0:T(8,128)(2,1)S(1)} %copy-done.17), kind=kOutput, calls=%fused_computation.43 | convolution fusion | flops 12888047616 | bytes 23068672 | tf_op jit(solution)/shard_map/pc,ctd->ptd/dot_general | solution.py:222
  503.0 3.4 copy.225
  509.8 20.2 %collective-permute-done.17 = bf16[2,3,128,512]{3,2,1,0:T(8,128)(2,1)S(1)} collective-permute-done((bf16[2,3,128,512]{3,2,1,0:T(8,128)(2,1)S(1)}, bf16[2,3,128,512]{3,2,1,0:T(8,128)(2,1)S(1)}, u32[]{:S(2)}, u32[]{:S(2)}) %collective-permute-start.17) | collective-permute-done | bytes 786464 | tf_op jit(solution)/shard_map/ppermute | solution.py:111
  531.9 9.0 %collective-permute-done.14 = bf16[3,128,512]{2,1,0:T(8,128)(2,1)S(1)} collective-permute-done((bf16[3,128,512]{2,1,0:T(8,128)(2,1)S(1)}, bf16[3,128,512]{2,1,0:T(8,128)(2,1)S(1)}, u32[]{:S(2)}, u32[]{:S(2)}) %collective-permute-start.14) | collective-permute-done | bytes 393248 | tf_op jit(solution)/shard_map/ppermute | solution.py:111
  541.0 8.2 %collective-permute-done.18 = bf16[3,128,512]{2,1,0:T(8,128)(2,1)S(1)} collective-permute-done((bf16[3,128,512]{2,1,0:T(8,128)(2,1)S(1)}, bf16[3,128,512]{2,1,0:T(8,128)(2,1)S(1)}, u32[]{:S(2)}, u32[]{:S(2)}) %collective-permute-start.18) | collective-permute-done | bytes 393248 | tf_op jit(solution)/shard_map/ppermute | solution.py:111
  (234 shorter events, 95.7 us)
Async XLA Ops:
  7.2 72.3 %copy-start = (bf16[512,2048]{1,0:T(8,128)(2,1)S(1)}, bf16[512,2048]{1,0:T(8,128)(2,1)}, u32[]{:S(2)}) copy-start(bf16[512,2048]{1,0:T(8,128)(2,1)} %param.19) | copy-start | bytes 6291460
  16.7 33.6 %all-to-all-start = ((f32[32,12,128]{2,1,0:T(8,128)}), f32[32,12,128]{2,1,0:T(8,128)S(1)}, u32[]{:S(2)}, u32[]{:S(2)}) async-start(f32[32,12,128]{2,1,0:T(8,128)} %broadcast_in_dim.30), calls=%async_computation | async-start | bytes 524288 | tf_op jit(solution)/shard_map/all_to_all | solution.py:42
  43.3 6.9 %copy-start.33 = (f32[2,512]{1,0:T(2,128)S(1)}, f32[2,512]{1,0:T(2,128)}, u32[]{:S(2)}) copy-start(f32[2,512]{1,0:T(2,128)} %param.20) | copy-start | bytes 12292
  43.3 6.9 %copy-start.35 = (f32[2,512]{1,0:T(2,128)S(1)}, f32[2,512]{1,0:T(2,128)}, u32[]{:S(2)}) copy-start(f32[2,512]{1,0:T(2,128)} %param.21) | copy-start | bytes 12292
  50.0 60.2 %collective-permute-start = (bf16[512,3,2048]{2,0,1:T(8,128)(2,1)}, bf16[512,3,2048]{2,0,1:T(8,128)(2,1)}, u32[]{:S(2)}, u32[]{:S(2)}) collective-permute-start(bf16[512,3,2048]{2,0,1:T(8,128)(2,1)} %fusion.9), channel_id=1, source_target_pairs={{0,1},{1,0},{2,3},{3,2},{4,5},{5,4},{6,7},{7,6},{8,9},{9,8},{10,11... | collective-permute-start | bytes 18874376 | tf_op jit(solution)/shard_map/ppermute | solution.py:115
  57.2 5.7 %copy-start.14 = (bf16[512,4608]{1,0:T(8,128)(2,1)}, bf16[512,4608]{1,0:T(8,128)(2,1)S(1)}, u32[]{:S(2)}) copy-start(bf16[512,4608]{1,0:T(8,128)(2,1)S(1)} %constant_dynamic-update-slice_fusion) | copy-start | bytes 14155780
  85.7 19.1 %all-to-all-start.2 = ((f32[32,32,128]{2,1,0:T(8,128)}), f32[32,32,128]{2,1,0:T(8,128)}, u32[]{:S(2)}, u32[]{:S(2)}) async-start(f32[32,32,128]{2,1,0:T(8,128)} %broadcast_in_dim.34), calls=%async_computation.2 | async-start | bytes 1048576 | tf_op jit(solution)/shard_map/all_to_all | solution.py:42
  89.3 20.2 %copy-start.30 = (f32[2048]{0:T(1024)S(1)}, f32[2048]{0:T(1024)}, u32[]{:S(2)}) copy-start(f32[2048]{0:T(1024)} %param.22) | copy-start | bytes 24580
  110.2 16.5 %copy-start.8 = (f32[2,16,16,2048]{3,2,1,0:T(8,128)S(1)}, f32[2,16,16,2048]{3,2,1,0:T(8,128)}, u32[]{:S(2)}) copy-start(f32[2,16,16,2048]{3,2,1,0:T(8,128)} %add_multiply_fusion) | copy-start | bytes 12582916
  130.4 9.4 %copy-start.6 = (f32[512,2048]{1,0:T(8,128)S(1)}, f32[512,2048]{1,0:T(8,128)}, u32[]{:S(2)}) copy-start(f32[512,2048]{1,0:T(8,128)} %copy-done.5) | copy-start | bytes 12582916
  130.4 9.4 %copy-start.11 = (bf16[2,16,16,2048]{3,2,1,0:T(8,128)(2,1)S(1)}, bf16[2,16,16,2048]{3,2,1,0:T(8,128)(2,1)}, u32[]{:S(2)}) copy-start(bf16[2,16,16,2048]{3,2,1,0:T(8,128)(2,1)} %param.13) | copy-start | bytes 6291460
  130.4 9.4 %copy-start.34 = (f32[2048]{0:T(1024)S(1)}, f32[2048]{0:T(1024)}, u32[]{:S(2)}) copy-start(f32[2048]{0:T(1024)} %param.23) | copy-start | bytes 24580
  155.3 18.9 %all-to-all-start.3 = ((f32[32,32,128]{2,1,0:T(8,128)}), f32[32,32,128]{2,1,0:T(8,128)}, u32[]{:S(2)}, u32[]{:S(2)}) async-start(f32[32,32,128]{2,1,0:T(8,128)} %broadcast_in_dim.36), calls=%async_computation.3 | async-start | bytes 1048576 | tf_op jit(solution)/shard_map/all_to_all | solution.py:42
  158.7 101.5 %all-gather.2.cloned.1.call-start = ((), (), s32[]{:S(2)}) async-start(), calls=%async_computation.6 | async-start | bytes 6291456 | tf_op jit(solution)/shard_map/all_gather | solution.py:196
  175.3 6.7 %copy-start.31 = (f32[2048]{0:T(1024)}, f32[2048]{0:T(1024)S(1)}, u32[]{:S(2)}) copy-start(f32[2048]{0:T(1024)S(1)} %get-tuple-element.144) | copy-start | bytes 24580
  175.3 6.7 %copy-start.32 = (f32[2048]{0:T(1024)}, f32[2048]{0:T(1024)S(1)}, u32[]{:S(2)}) copy-start(f32[2048]{0:T(1024)S(1)} %get-tuple-element.145) | copy-start | bytes 24580
  175.3 6.7 %copy-start.19 = (f32[512,512]{1,0:T(8,128)S(1)}, f32[512,512]{1,0:T(8,128)}, u32[]{:S(2)}) copy-start(f32[512,512]{1,0:T(8,128)} %copy-done.18) | copy-start | bytes 3145732
  185.5 20.0 %all-to-all-start.4 = ((f32[32,8,128]{2,1,0:T(8,128)}), f32[32,8,128]{2,1,0:T(8,128)S(1)}, u32[]{:S(2)}, u32[]{:S(2)}) async-start(f32[32,8,128]{2,1,0:T(8,128)} %broadcast_in_dim.38), calls=%async_computation.4 | async-start | bytes 262144 | tf_op jit(solution)/shard_map/all_to_all | solution.py:42
  199.5 6.0 %copy-start.20 = (f32[512,512]{1,0:T(8,128)S(1)}, f32[512,512]{1,0:T(8,128)}, u32[]{:S(2)}) copy-start(f32[512,512]{1,0:T(8,128)} %copy-done.18) | copy-start | bytes 3145732
  220.7 24.0 %all-to-all-start.5 = ((f32[32,8,128]{2,1,0:T(8,128)}), f32[32,8,128]{2,1,0:T(8,128)S(1)}, u32[]{:S(2)}, u32[]{:S(2)}) async-start(f32[32,8,128]{2,1,0:T(8,128)} %broadcast_in_dim.40), calls=%async_computation.5 | async-start | bytes 262144 | tf_op jit(solution)/shard_map/all_to_all | solution.py:42
  234.4 5.0 copy-start.7
  239.4 4.9 copy-start.2
  239.4 8.3 %copy-start.13 = (bf16[2048,512]{1,0:T(8,128)(2,1)S(1)}, bf16[2048,512]{1,0:T(8,128)(2,1)}, u32[]{:S(2)}) copy-start(bf16[2048,512]{1,0:T(8,128)(2,1)} %copy.211) | copy-start | bytes 6291460
  244.3 63.4 %collective-permute-start.6 = (bf16[2,2,2,2,208,512]{5,4,3,2,1,0:T(8,128)(2,1)}, bf16[2,2,2,2,208,512]{5,4,3,2,1,0:T(8,128)(2,1)}, u32[]{:S(2)}, u32[]{:S(2)}) collective-permute-start(bf16[2,2,2,2,208,512]{5,4,3,2,1,0:T(8,128)(2,1)} %fusion.22), channel_id=1, source_target_pairs={{0,1},{1,0},{2,3},{3,2},{4,5},{5,4},{6,7},{7,6},{8,9},{9,8},{10,11... | collective-permute-start | bytes 10223624 | tf_op jit(solution)/shard_map/ppermute | solution.py:115
  251.1 7.1 %collective-permute-start.1 = (bf16[2,2,2,2,64,512]{5,4,3,2,1,0:T(8,128)(2,1)S(1)}, bf16[2,2,2,2,64,512]{5,4,3,2,1,0:T(8,128)(2,1)S(1)}, u32[]{:S(2)}, u32[]{:S(2)}) collective-permute-start(bf16[2,2,2,2,64,512]{5,4,3,2,1,0:T(8,128)(2,1)S(1)} %fusion.49), channel_id=1, source_target_pairs={{0,1},{1,0},{2,3},{3,2},{4,5},{5,4},{6,7},{7,6},{8,9},{9,8},{10,11... | collective-permute-start | bytes 3145736 | tf_op jit(solution)/shard_map/ppermute | solution.py:115
  288.4 8.7 %copy-start.3 = (bf16[1024,2,2,2,2,128]{5,4,3,2,1,0:T(2,128)(2,1)S(1)}, bf16[1024,2,2,2,2,128]{5,4,3,2,1,0:T(2,128)(2,1)}, u32[]{:S(2)}) copy-start(bf16[1024,2,2,2,2,128]{5,4,3,2,1,0:T(2,128)(2,1)} %reshape.317) | copy-start | bytes 12582916
  295.2 137.7 %collective-permute-start.11 = (bf16[3,1024,512]{2,1,0:T(8,128)(2,1)}, bf16[3,1024,512]{2,1,0:T(8,128)(2,1)}, u32[]{:S(2)}, u32[]{:S(2)}) collective-permute-start(bf16[3,1024,512]{2,1,0:T(8,128)(2,1)} %convert_bitcast_fusion.1), channel_id=1, source_target_pairs={{0,2},{2,0},{4,6},{6,4},{8,10},{10,8},{12,14},{14,12},{16,18},{18,... | collective-permute-start | bytes 9437192 | tf_op jit(solution)/shard_map/ppermute | solution.py:111
  307.7 7.0 %copy-start.26 = (bf16[1024,2,2,1,2,128]{0,5,4,2,1,3:T(8,128)(2,1)S(1)}, bf16[1024,2,2,1,2,128]{0,5,4,2,1,3:T(8,128)(2,1)}, u32[]{:S(2)}) copy-start(bf16[1024,2,2,1,2,128]{0,5,4,2,1,3:T(8,128)(2,1)} %copy.222) | copy-start | bytes 6291460
  313.0 8.4 %copy-start.9 = (bf16[2,2,2,2,208,512]{5,4,3,2,1,0:T(8,128)(2,1)}, bf16[2,2,2,2,208,512]{5,4,3,2,1,0:T(8,128)(2,1)S(1)}, u32[]{:S(2)}) copy-start(bf16[2,2,2,2,208,512]{5,4,3,2,1,0:T(8,128)(2,1)S(1)} %fusion.8) | copy-start | bytes 10223620
  314.5 114.2 %collective-permute-start.7 = (bf16[2,2,2,208,512]{4,3,2,1,0:T(8,128)(2,1)}, bf16[2,2,2,208,512]{4,3,2,1,0:T(8,128)(2,1)}, u32[]{:S(2)}, u32[]{:S(2)}) collective-permute-start(bf16[2,2,2,208,512]{4,3,2,1,0:T(8,128)(2,1)} %dynamic-slice_bitcast_fusion), channel_id=1, source_target_pairs={{0,2},{2,0},{4,6},{6,4},{8,10},{10,8},{12,14},{14,12},{16,18},{18,... | collective-permute-start | bytes 5111816 | tf_op jit(solution)/shard_map/ppermute | solution.py:111
  321.4 119.0 %collective-permute-start.15 = (bf16[3,1024,512]{2,1,0:T(8,128)(2,1)}, bf16[3,1024,512]{2,1,0:T(8,128)(2,1)}, u32[]{:S(2)}, u32[]{:S(2)}) collective-permute-start(bf16[3,1024,512]{2,1,0:T(8,128)(2,1)} %convert_bitcast_fusion), channel_id=1, source_target_pairs={{0,4},{2,6},{4,0},{6,2},{8,12},{10,14},{12,8},{14,10},{16,20},{18,... | collective-permute-start | bytes 9437192 | tf_op jit(solution)/shard_map/ppermute | solution.py:111
  323.2 79.5 %collective-permute-start.2 = (bf16[2,2,2,64,512]{4,3,2,1,0:T(8,128)(2,1)S(1)}, bf16[2,2,2,64,512]{4,3,2,1,0:T(8,128)(2,1)S(1)}, u32[]{:S(2)}, u32[]{:S(2)}) collective-permute-start(bf16[2,2,2,64,512]{4,3,2,1,0:T(8,128)(2,1)S(1)} %dynamic-slice_bitcast_fusion.4), channel_id=1, source_target_pairs={{0,4},{2,6},{4,0},{6,2},{8,12},{10,14},{12,8},{14,10},{16,20},{18,... | collective-permute-start | bytes 1572872 | tf_op jit(solution)/shard_map/ppermute | solution.py:111
  403.7 7.4 %collective-permute-start.3 = (bf16[2,2,64,512]{3,2,1,0:T(8,128)(2,1)S(1)}, bf16[2,2,64,512]{3,2,1,0:T(8,128)(2,1)S(1)}, u32[]{:S(2)}, u32[]{:S(2)}) collective-permute-start(bf16[2,2,64,512]{3,2,1,0:T(8,128)(2,1)S(1)} %dynamic-slice_bitcast_fusion.8), channel_id=1, source_target_pairs={{0,2},{2,0},{4,6},{6,4},{8,10},{10,8},{12,14},{14,12},{16,18},{18,... | collective-permute-start | bytes 786440 | tf_op jit(solution)/shard_map/ppermute | solution.py:111
  412.1 40.1 %collective-permute-start.4 = (bf16[2,64,512]{2,1,0:T(8,128)(2,1)S(1)}, bf16[2,64,512]{2,1,0:T(8,128)(2,1)S(1)}, u32[]{:S(2)}, u32[]{:S(2)}) collective-permute-start(bf16[2,64,512]{2,1,0:T(8,128)(2,1)S(1)} %dynamic-slice_bitcast_fusion.10), channel_id=1, source_target_pairs={{0,8},{2,10},{4,12},{6,14},{8,0},{10,2},{12,4},{14,6},{16,24},{18,... | collective-permute-start | bytes 393224 | tf_op jit(solution)/shard_map/ppermute | solution.py:111
  428.6 4.3 copy-start.24
  431.3 9.2 %slice-start = ((s8[6291456]{0:T(1024)(128)(4,1)}), s8[4194304]{0:T(1024)(128)(4,1)S(1)}, s32[]{:S(2)}) async-start(s8[6291456]{0:T(1024)(128)(4,1)} %bitcast.335), calls=%async_computation.7 | async-start | bytes 8388608
  431.4 27.6 %collective-permute-start.8 = (bf16[2,2,208,512]{3,2,1,0:T(8,128)(2,1)S(1)}, bf16[2,2,208,512]{3,2,1,0:T(8,128)(2,1)S(1)}, u32[]{:S(2)}, u32[]{:S(2)}) collective-permute-start(bf16[2,2,208,512]{3,2,1,0:T(8,128)(2,1)S(1)} %dynamic-slice_bitcast_fusion.1), channel_id=1, source_target_pairs={{0,4},{2,6},{4,0},{6,2},{8,12},{10,14},{12,8},{14,10},{16,20},{18,... | collective-permute-start | bytes 2555912 | tf_op jit(solution)/shard_map/ppermute | solution.py:111
  432.9 7.5 %slice-start.1 = ((s8[6291456]{0:T(1024)(128)(4,1)}), s8[2097152]{0:T(1024)(128)(4,1)S(1)}, s32[]{:S(2)}) async-start(s8[6291456]{0:T(1024)(128)(4,1)} %bitcast.335), calls=%async_computation.8 | async-start | bytes 4194304
  439.6 43.9 %collective-permute-start.12 = (bf16[2,2,3,128,512]{4,3,2,0,1:T(8,128)(2,1)S(1)}, bf16[2,2,3,128,512]{4,3,2,0,1:T(8,128)(2,1)S(1)}, u32[]{:S(2)}, u32[]{:S(2)}) collective-permute-start(bf16[2,2,3,128,512]{4,3,2,0,1:T(8,128)(2,1)S(1)} %bitcast.360), channel_id=1, source_target_pairs={{0,4},{2,6},{4,0},{6,2},{8,12},{10,14},{12,8},{14,10},{16,20},{18,... | collective-permute-start | bytes 4718600 | tf_op jit(solution)/shard_map/ppermute | solution.py:111
  446.5 39.0 %collective-permute-start.16 = (bf16[2,2,3,128,512]{4,3,2,0,1:T(8,128)(2,1)S(1)}, bf16[2,2,3,128,512]{4,3,2,0,1:T(8,128)(2,1)S(1)}, u32[]{:S(2)}, u32[]{:S(2)}) collective-permute-start(bf16[2,2,3,128,512]{4,3,2,0,1:T(8,128)(2,1)S(1)} %bitcast.361), channel_id=1, source_target_pairs={{0,2},{2,0},{4,6},{6,4},{8,10},{10,8},{12,14},{14,12},{16,18},{18,... | collective-permute-start | bytes 4718600 | tf_op jit(solution)/shard_map/ppermute | solution.py:111
  452.3 5.9 %collective-permute-start.5 = (bf16[64,512]{1,0:T(8,128)(2,1)S(1)}, bf16[64,512]{1,0:T(8,128)(2,1)S(1)}, u32[]{:S(2)}, u32[]{:S(2)}) collective-permute-start(bf16[64,512]{1,0:T(8,128)(2,1)S(1)} %dynamic-slice_bitcast_fusion.11), channel_id=1, source_target_pairs={{0,16},{2,18},{4,20},{6,22},{8,24},{10,26},{12,28},{14,30},{16,0},... | collective-permute-start | bytes 196616 | tf_op jit(solution)/shard_map/ppermute | solution.py:111
  459.2 47.1 %collective-permute-start.9 = (bf16[2,208,512]{2,1,0:T(8,128)(2,1)S(1)}, bf16[2,208,512]{2,1,0:T(8,128)(2,1)S(1)}, u32[]{:S(2)}, u32[]{:S(2)}) collective-permute-start(bf16[2,208,512]{2,1,0:T(8,128)(2,1)S(1)} %dynamic-slice_bitcast_fusion.5), channel_id=1, source_target_pairs={{0,8},{2,10},{4,12},{6,14},{8,0},{10,2},{12,4},{14,6},{16,24},{18,... | collective-permute-start | bytes 1277960 | tf_op jit(solution)/shard_map/ppermute | solution.py:111
  484.2 24.8 %collective-permute-start.13 = (bf16[2,3,128,512]{3,2,1,0:T(8,128)(2,1)S(1)}, bf16[2,3,128,512]{3,2,1,0:T(8,128)(2,1)S(1)}, u32[]{:S(2)}, u32[]{:S(2)}) collective-permute-start(bf16[2,3,128,512]{3,2,1,0:T(8,128)(2,1)S(1)} %dynamic-slice_bitcast_fusion.3), channel_id=1, source_target_pairs={{0,8},{2,10},{4,12},{6,14},{8,0},{10,2},{12,4},{14,6},{16,24},{18,... | collective-permute-start | bytes 2359304 | tf_op jit(solution)/shard_map/ppermute | solution.py:111
  486.1 44.0 %collective-permute-start.17 = (bf16[2,3,128,512]{3,2,1,0:T(8,128)(2,1)S(1)}, bf16[2,3,128,512]{3,2,1,0:T(8,128)(2,1)S(1)}, u32[]{:S(2)}, u32[]{:S(2)}) collective-permute-start(bf16[2,3,128,512]{3,2,1,0:T(8,128)(2,1)S(1)} %dynamic-slice_bitcast_fusion.2), channel_id=1, source_target_pairs={{0,8},{2,10},{4,12},{6,14},{8,0},{10,2},{12,4},{14,6},{16,24},{18,... | collective-permute-start | bytes 2359304 | tf_op jit(solution)/shard_map/ppermute | solution.py:111
  506.5 23.9 %collective-permute-start.10 = (bf16[208,512]{1,0:T(8,128)(2,1)S(1)}, bf16[208,512]{1,0:T(8,128)(2,1)S(1)}, u32[]{:S(2)}, u32[]{:S(2)}) collective-permute-start(bf16[208,512]{1,0:T(8,128)(2,1)S(1)} %dynamic-slice_bitcast_fusion.9), channel_id=1, source_target_pairs={{0,16},{2,18},{4,20},{6,22},{8,24},{10,26},{12,28},{14,30},{16,0},... | collective-permute-start | bytes 638984 | tf_op jit(solution)/shard_map/ppermute | solution.py:111
  509.3 31.6 %collective-permute-start.14 = (bf16[3,128,512]{2,1,0:T(8,128)(2,1)S(1)}, bf16[3,128,512]{2,1,0:T(8,128)(2,1)S(1)}, u32[]{:S(2)}, u32[]{:S(2)}) collective-permute-start(bf16[3,128,512]{2,1,0:T(8,128)(2,1)S(1)} %dynamic-slice_bitcast_fusion.7), channel_id=1, source_target_pairs={{0,16},{2,18},{4,20},{6,22},{8,24},{10,26},{12,28},{14,30},{16,0},... | collective-permute-start | bytes 1179656 | tf_op jit(solution)/shard_map/ppermute | solution.py:111
  530.3 20.3 %copy-start.1 = (bf16[512,2048]{1,0:T(8,128)(2,1)S(1)}, bf16[512,2048]{1,0:T(8,128)(2,1)}, u32[]{:S(2)}) copy-start(bf16[512,2048]{1,0:T(8,128)(2,1)} %param.19) | copy-start | bytes 6291460
  530.3 18.9 %collective-permute-start.18 = (bf16[3,128,512]{2,1,0:T(8,128)(2,1)S(1)}, bf16[3,128,512]{2,1,0:T(8,128)(2,1)S(1)}, u32[]{:S(2)}, u32[]{:S(2)}) collective-permute-start(bf16[3,128,512]{2,1,0:T(8,128)(2,1)S(1)} %dynamic-slice_bitcast_fusion.6), channel_id=1, source_target_pairs={{0,16},{2,18},{4,20},{6,22},{8,24},{10,26},{12,28},{14,30},{16,0},... | collective-permute-start | bytes 1179656 | tf_op jit(solution)/shard_map/ppermute | solution.py:111
  (17 other events, 33.9 us)
Sparse Core Ops, SparseCore 0:
  169.4 14.8 all-gather.1
